TPU v7x, 512 devices: a whole 4x4x16 slice. The times are simulated.
512 devices in a mesh: dp: 16 (over z_hi, x), lat: 32 (over y, z_lo, core).
Axes of the slice: x: 4, y: 4, z: 16 (z_hi: 4, z_lo: 4; z = z_hi * 4 + z_lo), core: 2. Of those that a mesh axis runs over, the one named last changes fastest.
Arguments:
- states: bfloat16 [16, 128, 128, 128], P('dp', 'lat'), may hold values from -6 to 6
- basis_table: bfloat16 [128, 25, 9, 5], replicated, may hold values from -1.1953125 to 1.1953125
- offsets: int32 [128], replicated, may hold values from -12 to -8, as said below
- widths: int32 [128], replicated, may hold values from 21 to 25, as said below
- mixing: bfloat16 [9, 128, 128], replicated, may hold values from -0.1875 to 0.1875
- cotangent: bfloat16 [16, 128, 128, 128], P('dp', 'lat'), may hold values from -6 to 6
Outputs:
- output: bfloat16 [16, 128, 128, 128], P('dp', 'lat')
- grad_states: bfloat16 [16, 128, 128, 128], P('dp', 'lat')
- grad_mixing: float32 [9, 128, 128], replicated
Inputs may be any that keep to these rules, and one draw needn't show every extreme that they name: The support of every output latitude o contains o itself and lies within latitudes o - 12 to o + 12, so offsets[o] is at most 13 - widths[o]. widths is 25 at the two pole latitudes 0 and 127.
All inputs are finite; a program needn't handle non-finite values.
Results may differ from a plain program's by a relative error of at most 0.0049.
Values may be sent and summed in bfloat16 or wider, within the bound.
No kernel may reach another device: no remote copies, remote signals or barrier semaphores. Data moves between devices by JAX's collectives and lax.ppermute only.
A program may use at most 64 MiB of HBM per device.

v0:
```python
import math

import jax
import jax.numpy as jnp
from jax import lax
from jax.experimental import pallas as pl
from jax.experimental.pallas import tpu as pltpu
from jax.sharding import Mesh, PartitionSpec as P

TAPS = 5
GROUP = 4
WINDOW = GROUP + TAPS - 1
PART = 48
DP = ("z_hi", "x")
LAT = ("y", "z_lo", "core")
PLANE = ("x", "y", "core")
RING = ("z_hi", "z_lo")
SLOTS = ((-3, -2, -1, 0, 1, 2, 3), (3, -2, -3, 0, -1, 2, 1))
VMEM = pl.BlockSpec(memory_space=pltpu.VMEM)
SMEM = pl.BlockSpec(memory_space=pltpu.SMEM)
hold = lax.optimization_barrier


def call(kernel, outs, scratch, flops, *args, scalars=0):
    moved = sum(x.size * x.dtype.itemsize for x in tuple(args) + tuple(outs))
    return pl.pallas_call(
        kernel,
        out_shape=outs,
        in_specs=[SMEM] * scalars + [VMEM] * (len(args) - scalars),
        out_specs=[VMEM] * len(outs),
        scratch_shapes=scratch,
        compiler_params=pltpu.CompilerParams(vmem_limit_bytes=40 * 1024 * 1024),
        cost_estimate=pl.CostEstimate(flops=flops, bytes_accessed=moved, transcendentals=0),
    )(*args)


def by_longitude(x_ref, wide, rows, cells):
    for r in range(rows):
        wide[pl.ds(2 * rows + r, cells, stride=rows), :] = x_ref[r].astype(jnp.float32)
    edge = 2 * rows
    wide[0:edge, :] = wide[cells * rows : cells * rows + edge, :]
    wide[cells * rows + edge : cells * rows + 2 * edge, :] = wide[edge : 2 * edge, :]


def prepare_kernel(states_ref, cot_ref, both_out, own_out, wide):
    rows, cells, _ = states_ref.shape
    tall = wide.shape[0]
    by_longitude(states_ref, wide, rows, cells)
    both_out[:tall, :] = wide[...].astype(both_out.dtype)
    by_longitude(cot_ref, wide, rows, cells)
    both_out[tall:, :] = wide[...].astype(both_out.dtype)
    own_out[...] = wide[2 * rows : 2 * rows + cells * rows, :].astype(own_out.dtype)


def spread(rows, column, taken, out_ref):
    taps, pairs, latitudes = taken.shape
    height, width = out_ref.shape
    out_row = lax.broadcasted_iota(jnp.int32, (height, pairs), 0)
    pair = lax.broadcasted_iota(jnp.int32, (height, pairs), 1)
    block = GROUP * rows
    one = lambda x: x.astype(jnp.float32).astype(jnp.bfloat16)
    pick = one(out_row // block * rows + out_row % rows == pair)
    copy = one(lax.broadcasted_iota(jnp.int32, (latitudes, width), 0) == column)
    lane = lax.broadcasted_iota(jnp.int32, (height, width), 1)
    line = lax.broadcasted_iota(jnp.int32, (height, width), 0)
    step = lane // rows % WINDOW - line // rows % GROUP
    total = jnp.zeros((height, width), jnp.float32)
    for t in range(taps):
        tall = jnp.dot(pick, one(taken[t]), preferred_element_type=jnp.float32).astype(jnp.bfloat16)
        full = jnp.dot(tall, copy, preferred_element_type=jnp.float32)
        total = jnp.where(step == t, full, total)
    out_ref[...] = total.astype(out_ref.dtype)


def forward_table_kernel(rows, first_ref, offset_ref, width_ref, column_ref, table_ref, out_ref, padded, taken):
    basis, taps, support, latitudes = table_ref.shape
    depth = padded.shape[0] // taps
    slot = lax.broadcasted_iota(jnp.int32, (depth, latitudes), 0)
    latitude = lax.broadcasted_iota(jnp.int32, (depth, latitudes), 1)
    source = lax.broadcasted_iota(jnp.int32, (latitudes, latitudes), 0)
    first = first_ref[0]
    masks, spreads = [], []
    for q in range(rows):
        own = first + q
        masks.append((slot == latitude - own - offset_ref[own]) & (slot < width_ref[own]))
        spreads.append((source == own).astype(jnp.float32).astype(jnp.bfloat16))
    spreads = jnp.concatenate(spreads, axis=1)
    padded[...] = jnp.zeros_like(padded)
    taken[...] = jnp.zeros_like(taken)
    for k in range(basis):
        for t in range(taps):
            padded[t * depth : t * depth + support, :] = table_ref[k, t].astype(jnp.float32)
        every = jnp.dot(padded[...].astype(jnp.bfloat16), spreads, preferred_element_type=jnp.float32)
        for t in range(taps):
            for q in range(rows):
                values = every[t * depth : (t + 1) * depth, q * latitudes : (q + 1) * latitudes]
                row = jnp.sum(jnp.where(masks[q], values, 0.0), axis=0, keepdims=True)
                taken[t, k * rows + q : k * rows + q + 1, :] = row
    spread(rows, column_ref[...], taken, out_ref)


def adjoint_table_kernel(rows, first_ref, offset_ref, width_ref, column_ref, table_ref, out_ref, taken):
    basis, taps, support, latitudes = table_ref.shape
    slot = lax.broadcasted_iota(jnp.int32, (support, latitudes), 0)
    latitude = lax.broadcasted_iota(jnp.int32, (support, latitudes), 1)
    live = slot < width_ref[...]
    start = latitude + offset_ref[...]
    masks = [live & (slot == first_ref[0] + i - start) for i in range(rows)]
    taken[...] = jnp.zeros_like(taken)
    for k in range(basis):
        for t in range(taps):
            values = table_ref[k, t].astype(jnp.float32)
            for i in range(rows):
                row = jnp.sum(jnp.where(masks[i], values, 0.0), axis=0, keepdims=True)
                taken[taps - 1 - t, k * rows + i : k * rows + i + 1, :] = row
    spread(rows, column_ref[...], taken, out_ref)


def filter_bands(pieces, first, matrix, rows, basis, out_ref):
    block = GROUP * rows
    reach = WINDOW * rows
    channels = pieces[0].shape[1]
    groups = out_ref.shape[0] // block
    table = matrix[...]
    for g in range(0, groups, 2):
        halves = [
            jnp.concatenate([p[first + h * block : first + h * block + reach, :] for p in pieces], axis=0)
            for h in (g, g + 1)
        ]
        both = jnp.dot(
            table, jnp.concatenate(halves, axis=1), preferred_element_type=jnp.float32
        ).astype(out_ref.dtype)
        for half in range(2):
            for k in range(basis):
                out_ref[(g + half) * block : (g + half + 1) * block, k * channels : (k + 1) * channels] = both[
                    k * block : (k + 1) * block, half * channels : (half + 1) * channels
                ]


def forward_kernel(rows, *refs):
    pieces = refs[:7]
    matrix, own, filtered, grad = refs[7:]
    channels = own.shape[1]
    basis = filtered.shape[1] // channels
    filter_bands(pieces, 0, matrix, rows, basis, filtered)
    turned = lax.dot_general(
        own[...], filtered[...], (((0,), (0,)), ((), ())), preferred_element_type=jnp.float32
    )
    for k in range(basis):
        grad[k * channels : (k + 1) * channels, :] = turned[:, k * channels : (k + 1) * channels].T.astype(
            grad.dtype
        )
    used = basis * channels
    grad[used:, :] = jnp.zeros((grad.shape[0] - used, channels), grad.dtype)


def by_row(value, wide, out_ref):
    rows, cells, _ = out_ref.shape
    wide[...] = value
    for r in range(rows):
        out_ref[r] = wide[pl.ds(r, cells, stride=rows), :].astype(out_ref.dtype)


def backward_kernel(rows, *refs):
    pieces = refs[:7]
    matrix, filtered, mixing, output, grad_states, turned, wide = refs[7:]
    basis, channels, _ = mixing.shape
    by_row(
        jnp.dot(
            filtered[...],
            mixing[...].reshape(basis * channels, channels),
            preferred_element_type=jnp.float32,
        ),
        wide,
        output,
    )
    filter_bands(pieces, pieces[0].shape[0] // 2, matrix, rows, basis, turned)
    total = None
    for k in range(basis):
        term = lax.dot_general(
            turned[:, k * channels : (k + 1) * channels],
            mixing[k],
            (((1,), (1,)), ((), ())),
            preferred_element_type=jnp.float32,
        )
        total = term if total is None else total + term
    by_row(total, wide, grad_states)


def chips_apart(x):
    return lax.ppermute(x, LAT, steps(2)), lax.ppermute(x, LAT, steps(-2))


def far_and_near(x):
    far = [p for p in steps(3) if p[0] % 2 == 1] + [p for p in steps(-3) if p[0] % 2 == 0]
    return lax.ppermute(x, LAT, far), from_mate(x)


def from_mate(x):
    return lax.ppermute(x, LAT, [(i, i ^ 1) for i in range(lax.axis_size(LAT))])


def steps(by):
    count = lax.axis_size(LAT)
    return [(i, i + by) for i in range(count) if 0 <= i + by < count]


def scattered(parts):
    return lax.all_to_all(parts, PLANE, 0, 0).astype(jnp.float32).sum(0).astype(jnp.bfloat16)


def gathered(part, axes):
    return lax.all_to_all(jnp.broadcast_to(part[None], (lax.axis_size(axes),) + part.shape), axes, 0, 0)


def shards(states, basis_table, offsets, widths, mixing, cotangent):
    _, rows, cells, channels = states.shape
    basis = mixing.shape[0]
    first_row = lax.axis_index(LAT) * rows
    bf16 = jnp.bfloat16
    tall = jax.ShapeDtypeStruct((2 * (cells + TAPS - 1) * rows, channels), bf16)
    flat = jax.ShapeDtypeStruct((cells * rows, channels), bf16)
    both, cot_own = call(
        prepare_kernel,
        [tall, flat],
        [pltpu.VMEM((tall.shape[0] // 2, channels), jnp.float32)],
        0,
        states[0],
        cotangent[0],
    )
    before, after = chips_apart(both)
    far, mate = far_and_near(both)

    support, latitudes = basis_table.shape[1], basis_table.shape[0]
    table = basis_table.transpose(2, 3, 1, 0)
    band = jnp.where(lax.axis_index("core") == 0, jnp.array(SLOTS[0]), jnp.array(SLOTS[1]))
    column = first_row + band[:, None, None] * rows + jnp.arange(rows)[None, None, :]
    width = len(SLOTS[0]) * WINDOW * rows
    column = jnp.broadcast_to(column, (len(SLOTS[0]), WINDOW, rows)).reshape(1, width).astype(jnp.int32)
    matrix = jax.ShapeDtypeStruct((basis * GROUP * rows, width), bf16)
    first = first_row.astype(jnp.int32)[None]
    depth = -(-support // 8) * 8
    pairs = -(-basis * rows // 8) * 8
    taken = pltpu.VMEM((TAPS, pairs, latitudes), jnp.float32)
    (forward_wide,) = call(
        lambda *refs: forward_table_kernel(rows, *refs),
        [matrix],
        [pltpu.VMEM((TAPS * depth, latitudes), jnp.float32), taken],
        400_000_000,
        first,
        offsets,
        widths,
        column,
        table,
        scalars=3,
    )
    (adjoint_wide,) = call(
        lambda *refs: adjoint_table_kernel(rows, *refs),
        [matrix],
        [taken],
        400_000_000,
        first,
        offsets[None],
        widths[None],
        column,
        table,
        scalars=1,
    )

    before, after, forward_wide = hold((before, after, forward_wide))
    bands = (far, before, from_mate(before), both, mate, after, from_mate(after))
    plane = lax.axis_size(PLANE)
    filtered, grad = call(
        lambda *refs: forward_kernel(rows, *refs),
        [
            jax.ShapeDtypeStruct((cells * rows, basis * channels), bf16),
            jax.ShapeDtypeStruct((plane * PART, channels), bf16),
        ],
        [],
        2_000_000_000,
        *bands,
        forward_wide,
        cot_own,
    )
    part = scattered(grad.reshape(plane, PART, channels))
    part = gathered(part, RING).astype(jnp.float32).sum(0).astype(bf16)
    total = gathered(part, PLANE)
    output, grad_states = call(
        lambda *refs: backward_kernel(rows, *refs),
        [jax.ShapeDtypeStruct(states.shape[1:], bf16)] * 2,
        [
            pltpu.VMEM((cells * rows, basis * channels), bf16),
            pltpu.VMEM((cells * rows, channels), jnp.float32),
        ],
        3_000_000_000,
        *bands,
        adjoint_wide,
        filtered,
        mixing,
    )
    cell_count = lax.axis_size(DP) * rows * lax.axis_size(LAT) * cells
    grad_scale = 1.0 / math.sqrt(cell_count)
    whole = total.reshape(-1, channels)[: basis * channels].reshape(basis, channels, channels)
    return (output[None], grad_states[None], whole.astype(jnp.float32) * grad_scale)


def solution(mesh):
    fine = Mesh(mesh.devices.reshape(4, 4, 4, 4, 2), DP + LAT)
    banded = P(DP, LAT, None, None)
    in_specs = (banded, P(), P(), P(), P(), banded)
    out_specs = (banded, banded, P())
    return jax.shard_map(shards, mesh=fine, in_specs=in_specs, out_specs=out_specs, check_vma=False)
```

profile of v0, /device:TPU:1, one launch (start us, length us, event | category | flops | bytes accessed | tf_op | source)
XLA Modules:
  0.0 101.3 jit_solution(6323442962293218801)
XLA Ops:
  0.6 0.9 copy-done
  1.5 0.9 copy-done.1
  2.4 0.1 shard_map.103
  2.5 8.8 %collective-permute-start.4 = (bf16[1056,128]{1,0:T(8,128)(2,1)S(1)}, bf16[1056,128]{1,0:T(8,128)(2,1)S(1)}, u32[]{:S(2)}, u32[]{:S(2)}) collective-permute-start(bf16[1056,128]{1,0:T(8,128)(2,1)S(1)} %get-tuple-element.12.refs_3_), channel_id=1, source_target_pairs={{0,1},{1,0},{2,3},{3,2},{4,5},{5,4},{6,7},{7,6},{8,9},{9,8},{10,11... | collective-permute-start | bytes 811016 | tf_op jit(solution)/shard_map/ppermute | solution.py:200
  11.3 1.3 %collective-permute-start.2 = (bf16[1056,128]{1,0:T(8,128)(2,1)S(1)}, bf16[1056,128]{1,0:T(8,128)(2,1)S(1)}, u32[]{:S(2)}, u32[]{:S(2)}) collective-permute-start(bf16[1056,128]{1,0:T(8,128)(2,1)S(1)} %get-tuple-element.12.refs_3_), channel_id=1, source_target_pairs={{2,0},{3,1},{4,2},{5,3},{6,4},{7,5},{8,6},{9,7},{10,8},{11,9},{12,... | collective-permute-start | bytes 811016 | tf_op jit(solution)/shard_map/ppermute | solution.py:191
  12.6 4.0 %collective-permute-start.1 = (bf16[1056,128]{1,0:T(8,128)(2,1)S(1)}, bf16[1056,128]{1,0:T(8,128)(2,1)S(1)}, u32[]{:S(2)}, u32[]{:S(2)}) collective-permute-start(bf16[1056,128]{1,0:T(8,128)(2,1)S(1)} %get-tuple-element.12.refs_3_), channel_id=1, source_target_pairs={{0,2},{1,3},{2,4},{3,5},{4,6},{5,7},{6,8},{7,9},{8,10},{9,11},{10,... | collective-permute-start | bytes 811016 | tf_op jit(solution)/shard_map/ppermute | solution.py:191
  16.6 1.9 %collective-permute-start = (bf16[1056,128]{1,0:T(8,128)(2,1)S(1)}, bf16[1056,128]{1,0:T(8,128)(2,1)S(1)}, u32[]{:S(2)}, u32[]{:S(2)}) collective-permute-start(bf16[1056,128]{1,0:T(8,128)(2,1)S(1)} %get-tuple-element.12.refs_3_), channel_id=1, source_target_pairs={{1,4},{3,6},{5,8},{7,10},{9,12},{11,14},{13,16},{15,18},{17,20},{1... | collective-permute-start | bytes 811016 | tf_op jit(solution)/shard_map/ppermute | solution.py:196
  18.6 0.7 fusion.1
  19.2 0.1 iota_add_fusion
  19.3 0.1 reshape.44.refs_3_
  19.4 0.0 copy-start.2
  19.4 1.0 copy-done.2
  20.4 0.7 copy-done.5
  21.1 0.7 copy-done.7
  21.7 1.5 %shard_map.104.refs_7_ = bf16[144,224]{1,0:T(8,128)(2,1)S(1)} custom-call(s32[1]{0:T(128)} %bitcast.2.refs_0_, s32[128]{0:T(128)S(1)} %copy-done.5, s32[128]{0:T(128)S(1)} %copy-done.7, s32[1,224]{1,0:T(1,128)S(1)} %reshape.44.refs_3_, bf16[9,5,25,128]{3,2,1,0:T(8,128)(2,1)S(1)} %bitcast.13), custom_call_target="tpu_custom_call" | custom-call | flops 400000000 | bytes 354436 | tf_op jit(solution)/shard_map/pallas_call | solution.py:26
  23.3 3.9 %collective-permute-done.2.refs_5_ = bf16[1056,128]{1,0:T(8,128)(2,1)S(1)} collective-permute-done((bf16[1056,128]{1,0:T(8,128)(2,1)S(1)}, bf16[1056,128]{1,0:T(8,128)(2,1)S(1)}, u32[]{:S(2)}, u32[]{:S(2)}) %collective-permute-start.2) | collective-permute-done | bytes 270368 | tf_op jit(solution)/shard_map/ppermute | solution.py:191
  27.2 0.0 collective-permute-done.1.refs_1_
  27.2 2.7 %collective-permute-start.3 = (bf16[1056,128]{1,0:T(8,128)(2,1)S(1)}, bf16[1056,128]{1,0:T(8,128)(2,1)S(1)}, u32[]{:S(2)}, u32[]{:S(2)}) collective-permute-start(bf16[1056,128]{1,0:T(8,128)(2,1)S(1)} %collective-permute-done.1.refs_1_), channel_id=1, source_target_pairs={{0,1},{1,0},{2,3},{3,2},{4,5},{5,4},{6,7},{7,6},{8,9},{9,8},{10,11... | collective-permute-start | bytes 811016 | tf_op jit(solution)/shard_map/ppermute | solution.py:200
  29.9 1.9 %collective-permute-start.5 = (bf16[1056,128]{1,0:T(8,128)(2,1)S(1)}, bf16[1056,128]{1,0:T(8,128)(2,1)S(1)}, u32[]{:S(2)}, u32[]{:S(2)}) collective-permute-start(bf16[1056,128]{1,0:T(8,128)(2,1)S(1)} %collective-permute-done.2.refs_5_), channel_id=1, source_target_pairs={{0,1},{1,0},{2,3},{3,2},{4,5},{5,4},{6,7},{7,6},{8,9},{9,8},{10,11... | collective-permute-start | bytes 811016 | tf_op jit(solution)/shard_map/ppermute | solution.py:200
  31.9 4.8 %collective-permute-done.refs_0_ = bf16[1056,128]{1,0:T(8,128)(2,1)S(1)} collective-permute-done((bf16[1056,128]{1,0:T(8,128)(2,1)S(1)}, bf16[1056,128]{1,0:T(8,128)(2,1)S(1)}, u32[]{:S(2)}, u32[]{:S(2)}) %collective-permute-start) | collective-permute-done | bytes 270368 | tf_op jit(solution)/shard_map/ppermute | solution.py:196
  36.6 0.8 shard_map.106
  37.5 1.0 %copy-done.9 = bf16[512,1152]{1,0:T(8,128)(2,1)} copy-done((bf16[512,1152]{1,0:T(8,128)(2,1)}, bf16[512,1152]{1,0:T(8,128)(2,1)S(1)}, u32[]{:S(2)}) %copy-start.9) | copy-done | bytes 1179672
  38.5 17.8 %all_to_all.15 = bf16[32,48,128]{2,1,0:T(8,128)(2,1)S(1)} all-to-all(bf16[32,48,128]{2,1,0:T(8,128)(2,1)S(1)} %bitcast.10), channel_id=1, replica_groups=mesh['z_hi'=4,'x'=4,'y'=4,'z_lo'=4,'core'=2] {'x','y','core'}, dimensions={0} | all-to-all | bytes 786432 | tf_op jit(solution)/shard_map/all_to_all | solution.py:209
  56.3 0.1 reduce_sum.24
  56.4 25.7 %all_to_all.16 = bf16[16,48,128]{2,1,0:T(8,128)(2,1)S(1)} all-to-all(bf16[16,48,128]{2,1,0:T(8,128)(2,1)S(1)} %broadcast_in_dim.40), channel_id=1, replica_groups=mesh['z_hi'=4,'x'=4,'y'=4,'z_lo'=4,'core'=2] {'z_hi','z_lo'}, dimensions={0} | all-to-all | bytes 393216 | tf_op jit(solution)/shard_map/all_to_all | solution.py:213
  82.2 0.8 broadcast_in_dim.41
  83.0 7.1 %all-to-all-start.2 = ((bf16[32,48,128]{2,1,0:T(8,128)(2,1)}), bf16[32,48,128]{2,1,0:T(8,128)(2,1)S(1)}, u32[]{:S(2)}, u32[]{:S(2)}) async-start(bf16[32,48,128]{2,1,0:T(8,128)(2,1)} %broadcast_in_dim.41), calls=%async_computation.2 | async-start | bytes 786432 | tf_op jit(solution)/shard_map/all_to_all | solution.py:213
  90.1 0.7 shard_map.105.refs_7_
  90.9 0.5 copy-done.10
  91.4 1.9 %shard_map.107 = (bf16[4,128,128]{2,1,0:T(8,128)(2,1)}, bf16[4,128,128]{2,1,0:T(8,128)(2,1)}) custom-call(bf16[1056,128]{1,0:T(8,128)(2,1)S(1)} %collective-permute-done.refs_0_, bf16[1056,128]{1,0:T(8,128)(2,1)S(1)} %collective-permute-done.1.refs_1_, bf16[1056,128]{1,0:T(8,128)(2,1)S(1)} %collective-permute-done.3.refs_2_, ...), custom_call_target="tpu_custom_call" | custom-call | flops 3000000000 | bytes 3693568 | tf_op jit(solution)/shard_map/pallas_call | solution.py:26
  93.3 7.1 %all-to-all-done.2 = bf16[32,48,128]{2,1,0:T(8,128)(2,1)S(1)} async-done(((bf16[32,48,128]{2,1,0:T(8,128)(2,1)}), bf16[32,48,128]{2,1,0:T(8,128)(2,1)S(1)}, u32[]{:S(2)}, u32[]{:S(2)}) %all-to-all-start.2) | async-done | bytes 393248 | tf_op jit(solution)/shard_map/all_to_all | solution.py:213
  100.4 0.9 convert_multiply_fusion
  (20 shorter events, 0.1 us)
Async XLA Ops:
  0.6 0.9 copy-start
  1.5 0.9 copy-start.1
  2.5 29.3 %collective-permute-start.4 = (bf16[1056,128]{1,0:T(8,128)(2,1)S(1)}, bf16[1056,128]{1,0:T(8,128)(2,1)S(1)}, u32[]{:S(2)}, u32[]{:S(2)}) collective-permute-start(bf16[1056,128]{1,0:T(8,128)(2,1)S(1)} %get-tuple-element.12.refs_3_), channel_id=1, source_target_pairs={{0,1},{1,0},{2,3},{3,2},{4,5},{5,4},{6,7},{7,6},{8,9},{9,8},{10,11... | collective-permute-start | bytes 811016 | tf_op jit(solution)/shard_map/ppermute | solution.py:200
  11.3 15.9 %collective-permute-start.2 = (bf16[1056,128]{1,0:T(8,128)(2,1)S(1)}, bf16[1056,128]{1,0:T(8,128)(2,1)S(1)}, u32[]{:S(2)}, u32[]{:S(2)}) collective-permute-start(bf16[1056,128]{1,0:T(8,128)(2,1)S(1)} %get-tuple-element.12.refs_3_), channel_id=1, source_target_pairs={{2,0},{3,1},{4,2},{5,3},{6,4},{7,5},{8,6},{9,7},{10,8},{11,9},{12,... | collective-permute-start | bytes 811016 | tf_op jit(solution)/shard_map/ppermute | solution.py:191
  12.6 14.6 %collective-permute-start.1 = (bf16[1056,128]{1,0:T(8,128)(2,1)S(1)}, bf16[1056,128]{1,0:T(8,128)(2,1)S(1)}, u32[]{:S(2)}, u32[]{:S(2)}) collective-permute-start(bf16[1056,128]{1,0:T(8,128)(2,1)S(1)} %get-tuple-element.12.refs_3_), channel_id=1, source_target_pairs={{0,2},{1,3},{2,4},{3,5},{4,6},{5,7},{6,8},{7,9},{8,10},{9,11},{10,... | collective-permute-start | bytes 811016 | tf_op jit(solution)/shard_map/ppermute | solution.py:191
  16.6 20.0 %collective-permute-start = (bf16[1056,128]{1,0:T(8,128)(2,1)S(1)}, bf16[1056,128]{1,0:T(8,128)(2,1)S(1)}, u32[]{:S(2)}, u32[]{:S(2)}) collective-permute-start(bf16[1056,128]{1,0:T(8,128)(2,1)S(1)} %get-tuple-element.12.refs_3_), channel_id=1, source_target_pairs={{1,4},{3,6},{5,8},{7,10},{9,12},{11,14},{13,16},{15,18},{17,20},{1... | collective-permute-start | bytes 811016 | tf_op jit(solution)/shard_map/ppermute | solution.py:196
  19.4 1.0 copy-start.2
  20.4 0.7 copy-start.5
  21.1 0.7 copy-start.7
  27.2 9.4 %collective-permute-start.3 = (bf16[1056,128]{1,0:T(8,128)(2,1)S(1)}, bf16[1056,128]{1,0:T(8,128)(2,1)S(1)}, u32[]{:S(2)}, u32[]{:S(2)}) collective-permute-start(bf16[1056,128]{1,0:T(8,128)(2,1)S(1)} %collective-permute-done.1.refs_1_), channel_id=1, source_target_pairs={{0,1},{1,0},{2,3},{3,2},{4,5},{5,4},{6,7},{7,6},{8,9},{9,8},{10,11... | collective-permute-start | bytes 811016 | tf_op jit(solution)/shard_map/ppermute | solution.py:200
  29.9 6.7 %collective-permute-start.5 = (bf16[1056,128]{1,0:T(8,128)(2,1)S(1)}, bf16[1056,128]{1,0:T(8,128)(2,1)S(1)}, u32[]{:S(2)}, u32[]{:S(2)}) collective-permute-start(bf16[1056,128]{1,0:T(8,128)(2,1)S(1)} %collective-permute-done.2.refs_5_), channel_id=1, source_target_pairs={{0,1},{1,0},{2,3},{3,2},{4,5},{5,4},{6,7},{7,6},{8,9},{9,8},{10,11... | collective-permute-start | bytes 811016 | tf_op jit(solution)/shard_map/ppermute | solution.py:200
  37.5 1.0 %copy-start.9 = (bf16[512,1152]{1,0:T(8,128)(2,1)}, bf16[512,1152]{1,0:T(8,128)(2,1)S(1)}, u32[]{:S(2)}) copy-start(bf16[512,1152]{1,0:T(8,128)(2,1)S(1)} %get-tuple-element.17.refs_8_) | copy-start | bytes 3538948
  56.3 33.8 %copy-start.3 = (bf16[128,25,9,5]{0,1,3,2:T(8,128)(2,1)S(1)}, bf16[128,25,9,5]{0,1,3,2:T(8,128)(2,1)}, u32[]{:S(2)}) copy-start(bf16[128,25,9,5]{0,1,3,2:T(8,128)(2,1)} %param.9) | copy-start | bytes 864004
  56.3 33.8 %copy-start.6 = (s32[128]{0:T(128)S(1)}, s32[128]{0:T(128)}, u32[]{:S(2)}) copy-start(s32[128]{0:T(128)} %refs_1_.1) | copy-start | bytes 1540
  56.3 33.8 %copy-start.8 = (s32[128]{0:T(128)S(1)}, s32[128]{0:T(128)}, u32[]{:S(2)}) copy-start(s32[128]{0:T(128)} %refs_2_.1) | copy-start | bytes 1540
  83.0 7.9 %copy-start.4 = (bf16[9,128,128]{2,1,0:T(8,128)(2,1)S(1)}, bf16[9,128,128]{2,1,0:T(8,128)(2,1)}, u32[]{:S(2)}) copy-start(bf16[9,128,128]{2,1,0:T(8,128)(2,1)} %refs_9_.1) | copy-start | bytes 884740
  83.0 17.4 %all-to-all-start.2 = ((bf16[32,48,128]{2,1,0:T(8,128)(2,1)}), bf16[32,48,128]{2,1,0:T(8,128)(2,1)S(1)}, u32[]{:S(2)}, u32[]{:S(2)}) async-start(bf16[32,48,128]{2,1,0:T(8,128)(2,1)} %broadcast_in_dim.41), calls=%async_computation.2 | async-start | bytes 786432 | tf_op jit(solution)/shard_map/all_to_all | solution.py:213
  90.1 1.3 %copy-start.10 = (bf16[512,1152]{1,0:T(8,128)(2,1)S(1)}, bf16[512,1152]{1,0:T(8,128)(2,1)}, u32[]{:S(2)}) copy-start(bf16[512,1152]{1,0:T(8,128)(2,1)} %copy-done.9) | copy-start | bytes 3538948
where the time goes:
time: 102 us; the launch traced here: 101 us
  blocking collectives  43.5 us (43%)
  starting transfers between devices  27.7 us (27%)
  waiting for transfers between devices  15.9 us (16%)
  local copies, waits for them, and re-layouts  6.54 us (6%)
  Pallas kernels  5.09 us (5%)
  other arithmetic  1.71 us (2%)
    all_to_all x1, blocking collectives, gathered(): lax.all_to_all(jnp.broadcast_to(part[None], (lax.axis_size(axes),) + part...  25.7 us
    all_to_all x1, blocking collectives, scattered(): lax.all_to_all(parts, PLANE, 0, 0).astype(jnp.float32).sum(0)  17.8 us
    ppermute x3, starting transfers between devices, from_mate(): return lax.ppermute(x, LAT, [(i, i ^ 1) for i in range(lax.axis_size(LAT))])  13.4 us
    all_to_all x1, waiting for transfers between devices, gathered(): lax.all_to_all(jnp.broadcast_to(part[None], (lax.axis_size(axes),) + part...  7.13 us
    all_to_all x1, starting transfers between devices, gathered(): lax.all_to_all(jnp.broadcast_to(part[None], (lax.axis_size(axes),) + part...  7.1 us
    unnamed x22, local copies, waits for them, and re-layouts  5.61 us
    ppermute x2, starting transfers between devices, chips_apart(): return (lax.ppermute(x, LAT, steps(2)), lax.ppermute(x, LAT, steps(-2)))  5.29 us
    pallas_call x5, Pallas kernels, call(): pl.pallas_call(kernel, out_shape=outs, in_specs=[SMEM] * scalars + [VMEM]...  5.09 us
  transfers between devices with their start and end apart: 7, of which 3 were waited for; matrix products, arithmetic and copies ran while one was open for 1% of the time, Pallas kernels for 4%

commit v1 on v0

--- a/solution.py
+++ b/solution.py
@@ -10,7 +10,7 @@
 TAPS = 5
 GROUP = 4
 WINDOW = GROUP + TAPS - 1
-PART = 48
+PART = 40
 DP = ("z_hi", "x")
 LAT = ("y", "z_lo", "core")
 PLANE = ("x", "y", "core")
@@ -42,13 +42,12 @@
     wide[cells * rows + edge : cells * rows + 2 * edge, :] = wide[edge : 2 * edge, :]
 
 
-def prepare_kernel(states_ref, cot_ref, both_out, own_out, wide):
+def prepare_kernel(states_ref, cot_ref, states_out, cot_out, own_out, wide):
     rows, cells, _ = states_ref.shape
-    tall = wide.shape[0]
     by_longitude(states_ref, wide, rows, cells)
-    both_out[:tall, :] = wide[...].astype(both_out.dtype)
+    states_out[...] = wide[...].astype(states_out.dtype)
     by_longitude(cot_ref, wide, rows, cells)
-    both_out[tall:, :] = wide[...].astype(both_out.dtype)
+    cot_out[...] = wide[...].astype(cot_out.dtype)
     own_out[...] = wide[2 * rows : 2 * rows + cells * rows, :].astype(own_out.dtype)
 
 
@@ -139,7 +138,7 @@
 
 def forward_kernel(rows, *refs):
     pieces = refs[:7]
-    matrix, own, filtered, grad = refs[7:]
+    matrix, own, grad, filtered = refs[7:]
     channels = own.shape[1]
     basis = filtered.shape[1] // channels
     filter_bands(pieces, 0, matrix, rows, basis, filtered)
@@ -162,9 +161,10 @@
 
 
 def backward_kernel(rows, *refs):
-    pieces = refs[:7]
-    matrix, filtered, mixing, output, grad_states, turned, wide = refs[7:]
+    pieces, cot_pieces = refs[:7], refs[7:14]
+    forward, adjoint, mixing, output, grad_states, filtered, wide = refs[14:]
     basis, channels, _ = mixing.shape
+    filter_bands(pieces, 0, forward, rows, basis, filtered)
     by_row(
         jnp.dot(
             filtered[...],
@@ -174,11 +174,11 @@
         wide,
         output,
     )
-    filter_bands(pieces, pieces[0].shape[0] // 2, matrix, rows, basis, turned)
+    filter_bands(cot_pieces, 0, adjoint, rows, basis, filtered)
     total = None
     for k in range(basis):
         term = lax.dot_general(
-            turned[:, k * channels : (k + 1) * channels],
+            filtered[:, k * channels : (k + 1) * channels],
             mixing[k],
             (((1,), (1,)), ((), ())),
             preferred_element_type=jnp.float32,
@@ -218,18 +218,20 @@
     basis = mixing.shape[0]
     first_row = lax.axis_index(LAT) * rows
     bf16 = jnp.bfloat16
-    tall = jax.ShapeDtypeStruct((2 * (cells + TAPS - 1) * rows, channels), bf16)
+    tall = jax.ShapeDtypeStruct(((cells + TAPS - 1) * rows, channels), bf16)
     flat = jax.ShapeDtypeStruct((cells * rows, channels), bf16)
-    both, cot_own = call(
+    states_wide, cot_wide, cot_own = call(
         prepare_kernel,
-        [tall, flat],
-        [pltpu.VMEM((tall.shape[0] // 2, channels), jnp.float32)],
+        [tall, tall, flat],
+        [pltpu.VMEM(tall.shape, jnp.float32)],
         0,
         states[0],
         cotangent[0],
     )
-    before, after = chips_apart(both)
-    far, mate = far_and_near(both)
+    before, after = chips_apart(states_wide)
+    far, mate = far_and_near(states_wide)
+    cot_before, cot_after = chips_apart(cot_wide)
+    cot_far, cot_mate = far_and_near(cot_wide)
 
     support, latitudes = basis_table.shape[1], basis_table.shape[0]
     table = basis_table.transpose(2, 3, 1, 0)
@@ -268,15 +270,12 @@
     )
 
     before, after, forward_wide = hold((before, after, forward_wide))
-    bands = (far, before, from_mate(before), both, mate, after, from_mate(after))
+    bands = (far, before, from_mate(before), states_wide, mate, after, from_mate(after))
     plane = lax.axis_size(PLANE)
-    filtered, grad = call(
+    (grad,) = call(
         lambda *refs: forward_kernel(rows, *refs),
-        [
-            jax.ShapeDtypeStruct((cells * rows, basis * channels), bf16),
-            jax.ShapeDtypeStruct((plane * PART, channels), bf16),
-        ],
-        [],
+        [jax.ShapeDtypeStruct((plane * PART, channels), bf16)],
+        [pltpu.VMEM((cells * rows, basis * channels), bf16)],
         2_000_000_000,
         *bands,
         forward_wide,
@@ -285,6 +284,7 @@
     part = scattered(grad.reshape(plane, PART, channels))
     part = gathered(part, RING).astype(jnp.float32).sum(0).astype(bf16)
     total = gathered(part, PLANE)
+    cot_bands = (cot_far, cot_before, from_mate(cot_before), cot_wide, cot_mate, cot_after, from_mate(cot_after))
     output, grad_states = call(
         lambda *refs: backward_kernel(rows, *refs),
         [jax.ShapeDtypeStruct(states.shape[1:], bf16)] * 2,
@@ -294,8 +294,9 @@
         ],
         3_000_000_000,
         *bands,
+        *cot_bands,
+        forward_wide,
         adjoint_wide,
-        filtered,
         mixing,
     )
     cell_count = lax.axis_size(DP) * rows * lax.axis_size(LAT) * cells

time: 102 us -> 96.7 us (0.948)
  starting transfers between devices: 27.7 us -> 57.8 us
  blocking collectives: 43.5 us -> 17.5 us
  waiting for transfers between devices: 15.9 us -> 7.32 us
    all_to_all x1 -> x0, blocking collectives: 25.7 us -> none  [gathered(): lax.all_to_all(jnp.broadcast_to(part[None], (lax.axis_size(axes),) + part...]
    all_to_all x1 -> x2, starting transfers between devices: 7.1 us -> 20.7 us  [gathered(): lax.all_to_all(jnp.broadcast_to(part[None], (lax.axis_size(axes),) + part...]
    ppermute x3 -> x6, starting transfers between devices: 13.4 us -> 20.3 us  [from_mate(): return lax.ppermute(x, LAT, [(i, i ^ 1) for i in range(lax.axis_size(LAT))])]
    ppermute x2 -> x4, starting transfers between devices: 5.29 us -> 10.6 us  [chips_apart(): return (lax.ppermute(x, LAT, steps(2)), lax.ppermute(x, LAT, steps(-2)))]
    ppermute x1 -> x2, starting transfers between devices: 1.92 us -> 6.26 us  [far_and_near(): return (lax.ppermute(x, LAT, far), from_mate(x))]
    ppermute x2 -> x4, waiting for transfers between devices: 3.93 us -> 0.01 us  [chips_apart(): return (lax.ppermute(x, LAT, steps(2)), lax.ppermute(x, LAT, steps(-2)))]
    ppermute x1 -> x2, waiting for transfers between devices: 4.79 us -> 0.9 us  [far_and_near(): return (lax.ppermute(x, LAT, far), from_mate(x))]
    unnamed x22 -> x18, local copies, waits for them, and re-layouts: 5.61 us -> 4.27 us
  transfers between devices with their start and end apart: 7 -> 14, of which waited for: 3 -> 3; matrix products, arithmetic and copies ran while one was open for 1% -> 1% of each run, Pallas kernels for 4% -> 5%
where the time goes in v1:
time: 96.7 us; the launch traced here: 96 us
  starting transfers between devices  57.8 us (60%)
  blocking collectives  17.5 us (18%)
  waiting for transfers between devices  7.32 us (8%)
  local copies, waits for them, and re-layouts  5.84 us (6%)
  Pallas kernels  5.53 us (6%)
  other arithmetic  1.03 us (1%)
    all_to_all x2, starting transfers between devices, gathered(): lax.all_to_all(jnp.broadcast_to(part[None], (lax.axis_size(axes),) + part...  20.7 us
    ppermute x6, starting transfers between devices, from_mate(): return lax.ppermute(x, LAT, [(i, i ^ 1) for i in range(lax.axis_size(LAT))])  20.3 us
    all_to_all x1, blocking collectives, scattered(): lax.all_to_all(parts, PLANE, 0, 0).astype(jnp.float32).sum(0)  17.5 us
    ppermute x4, starting transfers between devices, chips_apart(): return (lax.ppermute(x, LAT, steps(2)), lax.ppermute(x, LAT, steps(-2)))  10.6 us
    all_to_all x2, waiting for transfers between devices, gathered(): lax.all_to_all(jnp.broadcast_to(part[None], (lax.axis_size(axes),) + part...  6.34 us
    ppermute x2, starting transfers between devices, far_and_near(): return (lax.ppermute(x, LAT, far), from_mate(x))  6.26 us
    pallas_call x5, Pallas kernels, call(): pl.pallas_call(kernel, out_shape=outs, in_specs=[SMEM] * scalars + [VMEM]...  5.53 us
    unnamed x18, local copies, waits for them, and re-layouts  4.27 us
  transfers between devices with their start and end apart: 14, of which 3 were waited for; matrix products, arithmetic and copies ran while one was open for 1% of the time, Pallas kernels for 5%

profile of v1, /device:TPU:1, one launch (start us, length us, event | category | flops | bytes accessed | tf_op | source)
XLA Modules:
  0.0 96.0 jit_solution(17771033758239799499)
XLA Ops:
  0.6 0.9 copy-done
  1.5 0.9 copy-done.1
  2.4 0.1 shard_map.103
  2.5 8.8 %collective-permute-start.4 = (bf16[528,128]{1,0:T(8,128)(2,1)S(1)}, bf16[528,128]{1,0:T(8,128)(2,1)S(1)}, u32[]{:S(2)}, u32[]{:S(2)}) collective-permute-start(bf16[528,128]{1,0:T(8,128)(2,1)S(1)} %get-tuple-element.11.refs_3_), channel_id=1, source_target_pairs={{0,1},{1,0},{2,3},{3,2},{4,5},{5,4},{6,7},{7,6},{8,9},{9,8},{10,11... | collective-permute-start | bytes 405512 | tf_op jit(solution)/shard_map/ppermute | solution.py:200
  11.3 1.3 %collective-permute-start.2 = (bf16[528,128]{1,0:T(8,128)(2,1)S(1)}, bf16[528,128]{1,0:T(8,128)(2,1)S(1)}, u32[]{:S(2)}, u32[]{:S(2)}) collective-permute-start(bf16[528,128]{1,0:T(8,128)(2,1)S(1)} %get-tuple-element.11.refs_3_), channel_id=1, source_target_pairs={{2,0},{3,1},{4,2},{5,3},{6,4},{7,5},{8,6},{9,7},{10,8},{11,9},{12,... | collective-permute-start | bytes 405512 | tf_op jit(solution)/shard_map/ppermute | solution.py:191
  12.6 4.0 %collective-permute-start.1 = (bf16[528,128]{1,0:T(8,128)(2,1)S(1)}, bf16[528,128]{1,0:T(8,128)(2,1)S(1)}, u32[]{:S(2)}, u32[]{:S(2)}) collective-permute-start(bf16[528,128]{1,0:T(8,128)(2,1)S(1)} %get-tuple-element.11.refs_3_), channel_id=1, source_target_pairs={{0,2},{1,3},{2,4},{3,5},{4,6},{5,7},{6,8},{7,9},{8,10},{9,11},{10,... | collective-permute-start | bytes 405512 | tf_op jit(solution)/shard_map/ppermute | solution.py:191
  16.6 1.9 %collective-permute-start = (bf16[528,128]{1,0:T(8,128)(2,1)S(1)}, bf16[528,128]{1,0:T(8,128)(2,1)S(1)}, u32[]{:S(2)}, u32[]{:S(2)}) collective-permute-start(bf16[528,128]{1,0:T(8,128)(2,1)S(1)} %get-tuple-element.11.refs_3_), channel_id=1, source_target_pairs={{1,4},{3,6},{5,8},{7,10},{9,12},{11,14},{13,16},{15,18},{17,20},{1... | collective-permute-start | bytes 405512 | tf_op jit(solution)/shard_map/ppermute | solution.py:196
  18.6 0.6 copy-done.7
  19.3 0.1 reshape.44.refs_3_
  19.5 0.6 copy-done.5
  20.1 1.0 %copy-done.2 = bf16[128,25,9,5]{0,1,3,2:T(8,128)(2,1)S(1)} copy-done((bf16[128,25,9,5]{0,1,3,2:T(8,128)(2,1)S(1)}, bf16[128,25,9,5]{0,1,3,2:T(8,128)(2,1)}, u32[]{:S(2)}) %copy-start.2) | copy-done | bytes 288024
  21.1 1.5 %shard_map.104.refs_14_.refs_7_ = bf16[144,224]{1,0:T(8,128)(2,1)S(1)} custom-call(s32[1]{0:T(128)} %bitcast.2.refs_0_, s32[128]{0:T(128)S(1)} %copy-done.5, s32[128]{0:T(128)S(1)} %copy-done.6, s32[1,224]{1,0:T(1,128)S(1)} %reshape.44.refs_3_, bf16[9,5,25,128]{3,2,1,0:T(8,128)(2,1)S(1)} %bitcast.14), custom_call_target="tpu_custom_call" | custom-call | flops 400000000 | bytes 354436 | tf_op jit(solution)/shard_map/pallas_call | solution.py:26
  22.7 1.9 %collective-permute-start.3 = (bf16[528,128]{1,0:T(8,128)(2,1)S(1)}, bf16[528,128]{1,0:T(8,128)(2,1)S(1)}, u32[]{:S(2)}, u32[]{:S(2)}) collective-permute-start(bf16[528,128]{1,0:T(8,128)(2,1)S(1)} %collective-permute-done.1.refs_1_), channel_id=1, source_target_pairs={{0,1},{1,0},{2,3},{3,2},{4,5},{5,4},{6,7},{7,6},{8,9},{9,8},{10,11... | collective-permute-start | bytes 405512 | tf_op jit(solution)/shard_map/ppermute | solution.py:200
  24.6 2.4 %collective-permute-start.5 = (bf16[528,128]{1,0:T(8,128)(2,1)S(1)}, bf16[528,128]{1,0:T(8,128)(2,1)S(1)}, u32[]{:S(2)}, u32[]{:S(2)}) collective-permute-start(bf16[528,128]{1,0:T(8,128)(2,1)S(1)} %collective-permute-done.2.refs_5_), channel_id=1, source_target_pairs={{0,1},{1,0},{2,3},{3,2},{4,5},{5,4},{6,7},{7,6},{8,9},{9,8},{10,11... | collective-permute-start | bytes 405512 | tf_op jit(solution)/shard_map/ppermute | solution.py:200
  27.0 0.9 collective-permute-done.refs_0_
  28.0 0.8 shard_map.107
  28.8 17.5 %all_to_all.15 = bf16[32,40,128]{2,1,0:T(8,128)(2,1)S(1)} all-to-all(bf16[32,40,128]{2,1,0:T(8,128)(2,1)S(1)} %bitcast.11), channel_id=1, replica_groups=mesh['z_hi'=4,'x'=4,'y'=4,'z_lo'=4,'core'=2] {'x','y','core'}, dimensions={0} | all-to-all | bytes 655360 | tf_op jit(solution)/shard_map/all_to_all | solution.py:209
  46.3 0.7 broadcast_in_dim.40
  47.0 12.8 %all-to-all-start.1 = ((bf16[16,40,128]{2,1,0:T(8,128)(2,1)}), bf16[16,40,128]{2,1,0:T(8,128)(2,1)S(1)}, u32[]{:S(2)}, u32[]{:S(2)}) async-start(bf16[16,40,128]{2,1,0:T(8,128)(2,1)} %broadcast_in_dim.40), calls=%async_computation.1 | async-start | bytes 327680 | tf_op jit(solution)/shard_map/all_to_all | solution.py:213
  59.9 1.3 %collective-permute-start.10 = (bf16[528,128]{1,0:T(8,128)(2,1)S(1)}, bf16[528,128]{1,0:T(8,128)(2,1)S(1)}, u32[]{:S(2)}, u32[]{:S(2)}) collective-permute-start(bf16[528,128]{1,0:T(8,128)(2,1)S(1)} %get-tuple-element.14.refs_10_), channel_id=1, source_target_pairs={{2,0},{3,1},{4,2},{5,3},{6,4},{7,5},{8,6},{9,7},{10,8},{11,9},{12,... | collective-permute-start | bytes 405512 | tf_op jit(solution)/shard_map/ppermute | solution.py:191
  61.2 4.0 %collective-permute-start.7 = (bf16[528,128]{1,0:T(8,128)(2,1)S(1)}, bf16[528,128]{1,0:T(8,128)(2,1)S(1)}, u32[]{:S(2)}, u32[]{:S(2)}) collective-permute-start(bf16[528,128]{1,0:T(8,128)(2,1)S(1)} %get-tuple-element.14.refs_10_), channel_id=1, source_target_pairs={{0,2},{1,3},{2,4},{3,5},{4,6},{5,7},{6,8},{7,9},{8,10},{9,11},{10,... | collective-permute-start | bytes 405512 | tf_op jit(solution)/shard_map/ppermute | solution.py:191
  65.2 2.8 %collective-permute-start.9 = (bf16[528,128]{1,0:T(8,128)(2,1)S(1)}, bf16[528,128]{1,0:T(8,128)(2,1)S(1)}, u32[]{:S(2)}, u32[]{:S(2)}) collective-permute-start(bf16[528,128]{1,0:T(8,128)(2,1)S(1)} %get-tuple-element.14.refs_10_), channel_id=1, source_target_pairs={{0,1},{1,0},{2,3},{3,2},{4,5},{5,4},{6,7},{7,6},{8,9},{9,8},{10,11... | collective-permute-start | bytes 405512 | tf_op jit(solution)/shard_map/ppermute | solution.py:200
  67.9 4.3 %collective-permute-start.6 = (bf16[528,128]{1,0:T(8,128)(2,1)S(1)}, bf16[528,128]{1,0:T(8,128)(2,1)S(1)}, u32[]{:S(2)}, u32[]{:S(2)}) collective-permute-start(bf16[528,128]{1,0:T(8,128)(2,1)S(1)} %get-tuple-element.14.refs_10_), channel_id=1, source_target_pairs={{1,4},{3,6},{5,8},{7,10},{9,12},{11,14},{13,16},{15,18},{17,20},{1... | collective-permute-start | bytes 405512 | tf_op jit(solution)/shard_map/ppermute | solution.py:196
  72.3 2.5 %collective-permute-start.11 = (bf16[528,128]{1,0:T(8,128)(2,1)S(1)}, bf16[528,128]{1,0:T(8,128)(2,1)S(1)}, u32[]{:S(2)}, u32[]{:S(2)}) collective-permute-start(bf16[528,128]{1,0:T(8,128)(2,1)S(1)} %collective-permute-done.10.refs_12_), channel_id=1, source_target_pairs={{0,1},{1,0},{2,3},{3,2},{4,5},{5,4},{6,7},{7,6},{8,9},{9,8},{10,11... | collective-permute-start | bytes 405512 | tf_op jit(solution)/shard_map/ppermute | solution.py:200
  74.8 1.9 %collective-permute-start.8 = (bf16[528,128]{1,0:T(8,128)(2,1)S(1)}, bf16[528,128]{1,0:T(8,128)(2,1)S(1)}, u32[]{:S(2)}, u32[]{:S(2)}) collective-permute-start(bf16[528,128]{1,0:T(8,128)(2,1)S(1)} %collective-permute-done.7.refs_8_), channel_id=1, source_target_pairs={{0,1},{1,0},{2,3},{3,2},{4,5},{5,4},{6,7},{7,6},{8,9},{9,8},{10,11... | collective-permute-start | bytes 405512 | tf_op jit(solution)/shard_map/ppermute | solution.py:200
  76.8 0.8 broadcast_in_dim.41
  77.5 7.9 %all-to-all-start.2 = ((bf16[32,40,128]{2,1,0:T(8,128)(2,1)}), bf16[32,40,128]{2,1,0:T(8,128)(2,1)S(1)}, u32[]{:S(2)}, u32[]{:S(2)}) async-start(bf16[32,40,128]{2,1,0:T(8,128)(2,1)} %broadcast_in_dim.41), calls=%async_computation.2 | async-start | bytes 655360 | tf_op jit(solution)/shard_map/all_to_all | solution.py:213
  85.5 0.7 shard_map.105.refs_15_
  86.3 0.2 copy-done.4
  86.4 2.3 %shard_map.106 = (bf16[4,128,128]{2,1,0:T(8,128)(2,1)}, bf16[4,128,128]{2,1,0:T(8,128)(2,1)}) custom-call(bf16[528,128]{1,0:T(8,128)(2,1)S(1)} %collective-permute-done.refs_0_, bf16[528,128]{1,0:T(8,128)(2,1)S(1)} %collective-permute-done.1.refs_1_, bf16[528,128]{1,0:T(8,128)(2,1)S(1)} %collective-permute-done.3.refs_2_, ...), custom_call_target="tpu_custom_call" | custom-call | flops 3000000000 | bytes 2578432 | tf_op jit(solution)/shard_map/pallas_call | solution.py:26
  88.8 6.3 %all-to-all-done.2 = bf16[32,40,128]{2,1,0:T(8,128)(2,1)S(1)} async-done(((bf16[32,40,128]{2,1,0:T(8,128)(2,1)}), bf16[32,40,128]{2,1,0:T(8,128)(2,1)S(1)}, u32[]{:S(2)}, u32[]{:S(2)}) %all-to-all-start.2) | async-done | bytes 327712 | tf_op jit(solution)/shard_map/all_to_all | solution.py:213
  95.1 0.9 convert_multiply_fusion
  (29 shorter events, 0.3 us)
Async XLA Ops:
  0.6 0.9 copy-start
  1.5 0.9 copy-start.1
  2.5 24.5 %collective-permute-start.4 = (bf16[528,128]{1,0:T(8,128)(2,1)S(1)}, bf16[528,128]{1,0:T(8,128)(2,1)S(1)}, u32[]{:S(2)}, u32[]{:S(2)}) collective-permute-start(bf16[528,128]{1,0:T(8,128)(2,1)S(1)} %get-tuple-element.11.refs_3_), channel_id=1, source_target_pairs={{0,1},{1,0},{2,3},{3,2},{4,5},{5,4},{6,7},{7,6},{8,9},{9,8},{10,11... | collective-permute-start | bytes 405512 | tf_op jit(solution)/shard_map/ppermute | solution.py:200
  11.3 11.3 %collective-permute-start.2 = (bf16[528,128]{1,0:T(8,128)(2,1)S(1)}, bf16[528,128]{1,0:T(8,128)(2,1)S(1)}, u32[]{:S(2)}, u32[]{:S(2)}) collective-permute-start(bf16[528,128]{1,0:T(8,128)(2,1)S(1)} %get-tuple-element.11.refs_3_), channel_id=1, source_target_pairs={{2,0},{3,1},{4,2},{5,3},{6,4},{7,5},{8,6},{9,7},{10,8},{11,9},{12,... | collective-permute-start | bytes 405512 | tf_op jit(solution)/shard_map/ppermute | solution.py:191
  12.6 10.0 %collective-permute-start.1 = (bf16[528,128]{1,0:T(8,128)(2,1)S(1)}, bf16[528,128]{1,0:T(8,128)(2,1)S(1)}, u32[]{:S(2)}, u32[]{:S(2)}) collective-permute-start(bf16[528,128]{1,0:T(8,128)(2,1)S(1)} %get-tuple-element.11.refs_3_), channel_id=1, source_target_pairs={{0,2},{1,3},{2,4},{3,5},{4,6},{5,7},{6,8},{7,9},{8,10},{9,11},{10,... | collective-permute-start | bytes 405512 | tf_op jit(solution)/shard_map/ppermute | solution.py:191
  16.6 11.3 %collective-permute-start = (bf16[528,128]{1,0:T(8,128)(2,1)S(1)}, bf16[528,128]{1,0:T(8,128)(2,1)S(1)}, u32[]{:S(2)}, u32[]{:S(2)}) collective-permute-start(bf16[528,128]{1,0:T(8,128)(2,1)S(1)} %get-tuple-element.11.refs_3_), channel_id=1, source_target_pairs={{1,4},{3,6},{5,8},{7,10},{9,12},{11,14},{13,16},{15,18},{17,20},{1... | collective-permute-start | bytes 405512 | tf_op jit(solution)/shard_map/ppermute | solution.py:196
  18.6 0.7 copy-start.7
  18.6 0.7 copy-start.8
  19.4 0.7 copy-start.5
  19.4 0.7 copy-start.6
  20.1 1.0 %copy-start.2 = (bf16[128,25,9,5]{0,1,3,2:T(8,128)(2,1)S(1)}, bf16[128,25,9,5]{0,1,3,2:T(8,128)(2,1)}, u32[]{:S(2)}) copy-start(bf16[128,25,9,5]{0,1,3,2:T(8,128)(2,1)} %param.9) | copy-start | bytes 864004
  22.7 5.2 %collective-permute-start.3 = (bf16[528,128]{1,0:T(8,128)(2,1)S(1)}, bf16[528,128]{1,0:T(8,128)(2,1)S(1)}, u32[]{:S(2)}, u32[]{:S(2)}) collective-permute-start(bf16[528,128]{1,0:T(8,128)(2,1)S(1)} %collective-permute-done.1.refs_1_), channel_id=1, source_target_pairs={{0,1},{1,0},{2,3},{3,2},{4,5},{5,4},{6,7},{7,6},{8,9},{9,8},{10,11... | collective-permute-start | bytes 405512 | tf_op jit(solution)/shard_map/ppermute | solution.py:200
  24.6 3.4 %collective-permute-start.5 = (bf16[528,128]{1,0:T(8,128)(2,1)S(1)}, bf16[528,128]{1,0:T(8,128)(2,1)S(1)}, u32[]{:S(2)}, u32[]{:S(2)}) collective-permute-start(bf16[528,128]{1,0:T(8,128)(2,1)S(1)} %collective-permute-done.2.refs_5_), channel_id=1, source_target_pairs={{0,1},{1,0},{2,3},{3,2},{4,5},{5,4},{6,7},{7,6},{8,9},{9,8},{10,11... | collective-permute-start | bytes 405512 | tf_op jit(solution)/shard_map/ppermute | solution.py:200
  47.0 29.7 %all-to-all-start.1 = ((bf16[16,40,128]{2,1,0:T(8,128)(2,1)}), bf16[16,40,128]{2,1,0:T(8,128)(2,1)S(1)}, u32[]{:S(2)}, u32[]{:S(2)}) async-start(bf16[16,40,128]{2,1,0:T(8,128)(2,1)} %broadcast_in_dim.40), calls=%async_computation.1 | async-start | bytes 327680 | tf_op jit(solution)/shard_map/all_to_all | solution.py:213
  59.9 12.4 %collective-permute-start.10 = (bf16[528,128]{1,0:T(8,128)(2,1)S(1)}, bf16[528,128]{1,0:T(8,128)(2,1)S(1)}, u32[]{:S(2)}, u32[]{:S(2)}) collective-permute-start(bf16[528,128]{1,0:T(8,128)(2,1)S(1)} %get-tuple-element.14.refs_10_), channel_id=1, source_target_pairs={{2,0},{3,1},{4,2},{5,3},{6,4},{7,5},{8,6},{9,7},{10,8},{11,9},{12,... | collective-permute-start | bytes 405512 | tf_op jit(solution)/shard_map/ppermute | solution.py:191
  61.2 13.6 %collective-permute-start.7 = (bf16[528,128]{1,0:T(8,128)(2,1)S(1)}, bf16[528,128]{1,0:T(8,128)(2,1)S(1)}, u32[]{:S(2)}, u32[]{:S(2)}) collective-permute-start(bf16[528,128]{1,0:T(8,128)(2,1)S(1)} %get-tuple-element.14.refs_10_), channel_id=1, source_target_pairs={{0,2},{1,3},{2,4},{3,5},{4,6},{5,7},{6,8},{7,9},{8,10},{9,11},{10,... | collective-permute-start | bytes 405512 | tf_op jit(solution)/shard_map/ppermute | solution.py:191
  65.2 21.1 %collective-permute-start.9 = (bf16[528,128]{1,0:T(8,128)(2,1)S(1)}, bf16[528,128]{1,0:T(8,128)(2,1)S(1)}, u32[]{:S(2)}, u32[]{:S(2)}) collective-permute-start(bf16[528,128]{1,0:T(8,128)(2,1)S(1)} %get-tuple-element.14.refs_10_), channel_id=1, source_target_pairs={{0,1},{1,0},{2,3},{3,2},{4,5},{5,4},{6,7},{7,6},{8,9},{9,8},{10,11... | collective-permute-start | bytes 405512 | tf_op jit(solution)/shard_map/ppermute | solution.py:200
  67.9 18.3 %collective-permute-start.6 = (bf16[528,128]{1,0:T(8,128)(2,1)S(1)}, bf16[528,128]{1,0:T(8,128)(2,1)S(1)}, u32[]{:S(2)}, u32[]{:S(2)}) collective-permute-start(bf16[528,128]{1,0:T(8,128)(2,1)S(1)} %get-tuple-element.14.refs_10_), channel_id=1, source_target_pairs={{1,4},{3,6},{5,8},{7,10},{9,12},{11,14},{13,16},{15,18},{17,20},{1... | collective-permute-start | bytes 405512 | tf_op jit(solution)/shard_map/ppermute | solution.py:196
  72.3 14.0 %collective-permute-start.11 = (bf16[528,128]{1,0:T(8,128)(2,1)S(1)}, bf16[528,128]{1,0:T(8,128)(2,1)S(1)}, u32[]{:S(2)}, u32[]{:S(2)}) collective-permute-start(bf16[528,128]{1,0:T(8,128)(2,1)S(1)} %collective-permute-done.10.refs_12_), channel_id=1, source_target_pairs={{0,1},{1,0},{2,3},{3,2},{4,5},{5,4},{6,7},{7,6},{8,9},{9,8},{10,11... | collective-permute-start | bytes 405512 | tf_op jit(solution)/shard_map/ppermute | solution.py:200
  74.8 11.5 %collective-permute-start.8 = (bf16[528,128]{1,0:T(8,128)(2,1)S(1)}, bf16[528,128]{1,0:T(8,128)(2,1)S(1)}, u32[]{:S(2)}, u32[]{:S(2)}) collective-permute-start(bf16[528,128]{1,0:T(8,128)(2,1)S(1)} %collective-permute-done.7.refs_8_), channel_id=1, source_target_pairs={{0,1},{1,0},{2,3},{3,2},{4,5},{5,4},{6,7},{7,6},{8,9},{9,8},{10,11... | collective-permute-start | bytes 405512 | tf_op jit(solution)/shard_map/ppermute | solution.py:200
  77.5 7.9 %copy-start.3 = (bf16[128,25,9,5]{0,1,3,2:T(8,128)(2,1)S(1)}, bf16[128,25,9,5]{0,1,3,2:T(8,128)(2,1)}, u32[]{:S(2)}) copy-start(bf16[128,25,9,5]{0,1,3,2:T(8,128)(2,1)} %param.9) | copy-start | bytes 864004
  77.5 17.6 %all-to-all-start.2 = ((bf16[32,40,128]{2,1,0:T(8,128)(2,1)}), bf16[32,40,128]{2,1,0:T(8,128)(2,1)S(1)}, u32[]{:S(2)}, u32[]{:S(2)}) async-start(bf16[32,40,128]{2,1,0:T(8,128)(2,1)} %broadcast_in_dim.41), calls=%async_computation.2 | async-start | bytes 655360 | tf_op jit(solution)/shard_map/all_to_all | solution.py:213
  85.5 1.0 %copy-start.4 = (bf16[9,128,128]{2,1,0:T(8,128)(2,1)S(1)}, bf16[9,128,128]{2,1,0:T(8,128)(2,1)}, u32[]{:S(2)}) copy-start(bf16[9,128,128]{2,1,0:T(8,128)(2,1)} %refs_16_.1) | copy-start | bytes 884740
